TPU v7x, 256 devices: a whole 4x4x8 slice. The times are simulated.
256 devices in a mesh: phase: 4 (over x), dom: 64 (over y, z, core).
Axes of the slice: x: 4, y: 4, z: 8, core: 2. Of those that a mesh axis runs over, the one named last changes fastest.
Arguments:
- edges_fwd: bfloat16 [4, 49152, 256], P('phase', 'dom'), may hold values from -6 to 6
- nodes_fwd: bfloat16 [4, 65536, 256], P('phase', 'dom'), may hold values from -6 to 6
- edges_stash: bfloat16 [4, 49152, 256], P('phase', 'dom'), may hold values from -6 to 6
- nodes_stash: bfloat16 [4, 65536, 256], P('phase', 'dom'), may hold values from -6 to 6
- edge_cot: bfloat16 [4, 49152, 256], P('phase', 'dom'), may hold values from -6 to 6
- node_cot: bfloat16 [4, 65536, 256], P('phase', 'dom'), may hold values from -6 to 6
- edge_w1: bfloat16 [4, 768, 256], P('phase'), may hold values from -0.21875 to 0.21875
- edge_w2: bfloat16 [4, 256, 256], P('phase'), may hold values from -0.375 to 0.375
- edge_vectors: float32 [4, 4, 256], P('phase'), may hold values from -2 to 2
- node_w1: bfloat16 [4, 512, 256], P('phase'), may hold values from -0.25 to 0.25
- node_w2: bfloat16 [4, 256, 256], P('phase'), may hold values from -0.375 to 0.375
- node_vectors: float32 [4, 4, 256], P('phase'), may hold values from -2 to 2
- edge_nodes: int32 [2, 49152], P(None, 'dom'), may hold values from 0 to 1535, as said below
- mirror_rows: int32 [64, 64, 8], P('dom'), may hold values from 0 to 1023
- edge_count: int32 [64], P('dom'), may hold values from 1 to 768, 30720 in all
Outputs:
- next_edges: bfloat16 [4, 49152, 256], P('phase', 'dom')
- next_nodes: bfloat16 [4, 65536, 256], P('phase', 'dom')
- prev_edge_grads: bfloat16 [4, 49152, 256], P('phase', 'dom')
- prev_node_grads: bfloat16 [4, 65536, 256], P('phase', 'dom')
- grad_edge_w1: float32 [4, 768, 256], P('phase')
- grad_edge_w2: float32 [4, 256, 256], P('phase')
- grad_edge_vectors: float32 [4, 4, 256], P('phase')
- grad_node_w1: float32 [4, 512, 256], P('phase')
- grad_node_w2: float32 [4, 256, 256], P('phase')
- grad_node_vectors: float32 [4, 4, 256], P('phase')
Inputs may be any that keep to these rules, and one draw needn't show every extreme that they name: `edge_nodes`: columns d * 768 to (d + 1) * 768 - 1 belong to dom index d and name rows of its node table. In each aligned block of 128 edge slots, all receivers lie in one tile of 128 table rows and all senders in one tile. `mirror_rows`: entry [p, d, c] is the row of owner p's nodes that dom index d holds as its mirrored row c of owner p. The live edges of dom index d are its first edge_count[d] edge slots.
All inputs are finite; a program needn't handle non-finite values. No bound on the sum of `edge_count` on one device may be relied on, other than what follows from the above.
Results may differ from a plain program's by a relative error of at most 0.024.
The roundings to bfloat16 on the way count: a program that leaves them out, or rounds other values in their place, can miss the bound.
Values may be sent and summed in bfloat16 or wider, within the bound.
A program may use at most 64 MiB of HBM per device.

v0:
```python
import jax
import jax.numpy as jnp
from jax import lax
from jax.experimental import pallas as pl
from jax.experimental.pallas import tpu as pltpu
from jax.sharding import PartitionSpec as P

TILE = 128
EPSILON = 1e-05
Z_SIZE = 8
GROUP = 8
F32 = jnp.float32
BF16 = jnp.bfloat16
MESH = pl.DeviceIdType.MESH
CHUNK = 256


def dot(a, b, contract=((1,), (0,))):
    return lax.dot_general(a, b, (contract, ((), ())), preferred_element_type=F32)


def dot_nt(a, b):
    return dot(a, b, ((1,), (1,)))


def dot_tn(a, b):
    return dot(a, b, ((0,), (0,)))


def layer_norm(pre_norm):
    row_mean = jnp.mean(pre_norm, axis=-1, keepdims=True)
    centered = pre_norm - row_mean
    row_var = jnp.mean(centered * centered, axis=-1, keepdims=True)
    inverse = lax.rsqrt(row_var + EPSILON)
    return centered * inverse, inverse


def norm_back(scaled, normed, inverse):
    mean_first = jnp.mean(scaled, axis=-1, keepdims=True)
    mean_second = jnp.mean(scaled * normed, axis=-1, keepdims=True)
    return inverse * (scaled - mean_first - normed * mean_second)


def to_slabs(rows):
    count = rows.shape[0] // 8
    left = rows[:, :128].reshape(count, 8, 128)
    right = rows[:, 128:].reshape(count, 8, 128)
    return jnp.concatenate([left, right], axis=1).astype(BF16)


def from_slabs(slabs):
    wide = slabs.astype(F32)
    count = wide.shape[0]
    left = wide[:, :8, :].reshape(count * 8, 128)
    right = wide[:, 8:, :].reshape(count * 8, 128)
    return jnp.concatenate([left, right], axis=1).astype(BF16)


def col_sum(rows):
    return jnp.sum(rows, axis=0, keepdims=True)


def rows_at(i, size=CHUNK):
    return pl.ds(pl.multiple_of(i * size, size), size)


def tick_kernel(
    dom_count,
    phase_count,
    ef, nf, es, ns, ec, nc, w1, w2, ev, nw1, nw2, nv, idx, sidx, cnt,
    o_ne, o_nn, o_pe, o_pn, o_ge, o_gn, o_gv,
    send_hot, send_hot_t, recv_hot, recv_hot_t, want_hot, want_hot_t,
    table_s, table_f, table_g, out_slab, in_slab,
    sent_rows, recv_rows, edge_pre, edge_hid, edge_norm, edge_inv, edge_pre_grad, edge_first_grad,
    node_pre, node_hid, node_norm, node_inv, agg_rows, node_first_grad, node_pre_grad,
    block_sums, own_s, own_f, base,
    new_edges, new_nodes, old_edges, old_nodes,
    g_edge, g_node, ra_edge, ra_node, sb, rb, fb, ab, va, vb, vec,
    x_send, x_recv, sh_send, sh_recv, ra_s, ra_r, rb_s, rb_r, gb_s, gb_r, ga_s, ga_r, v_s, v_r, local_sem,
):
    me = lax.axis_index("dom")
    phase = lax.axis_index("phase")
    zpos = lax.rem(me // 2, Z_SIZE)
    apos = (me // (2 * Z_SIZE)) * 2 + lax.rem(me, 2)
    features = ef.shape[1]
    node_dev = nf.shape[0]
    edge_dev = ef.shape[0]
    blocks = edge_dev // TILE
    own_tiles = node_dev // TILE
    mirror_tiles = (dom_count * 8) // TILE
    node_chunks = node_dev // CHUNK
    edge_chunks = edge_dev // CHUNK
    per_chunk = CHUNK // TILE

    def a_partner(k):
        other = lax.rem(apos + k, GROUP)
        return other, (other // 2) * (2 * Z_SIZE) + zpos * 2 + lax.rem(other, 2)

    def b_partner(k):
        other = lax.rem(zpos + k, Z_SIZE)
        return other, me + 2 * (other - zpos)

    barrier = pltpu.get_barrier_semaphore()

    def greet(k, carry):
        pl.semaphore_signal(
            barrier, inc=1, device_id={"dom": lax.rem(me + k, dom_count)}, device_id_type=MESH
        )
        return carry

    lax.fori_loop(1, dom_count, greet, 0)
    for step in (1, phase_count - 1):
        pl.semaphore_signal(
            barrier, inc=1, device_id={"phase": lax.rem(phase + step, phase_count)}, device_id_type=MESH
        )

    def start_exchange(x):
        def one(k, carry):
            other = lax.rem(me + k, dom_count)
            pltpu.make_async_remote_copy(
                out_slab.at[x, other], in_slab.at[x, me], x_send.at[x], x_recv.at[x],
                device_id={"dom": other}, device_id_type=MESH,
            ).start()
            return carry

        lax.fori_loop(1, dom_count, one, 0)
        in_slab[x, me] = out_slab[x, me]

    def exchange_all(x):
        part = pl.ds(0, dom_count - 1)
        return pltpu.make_async_remote_copy(
            out_slab.at[x, part], in_slab.at[x, part], x_send.at[x], x_recv.at[x],
            device_id={"dom": lax.rem(me + 1, dom_count)}, device_id_type=MESH,
        )

    def wait_exchange(x):
        exchange_all(x).wait_recv()
        return from_slabs(in_slab[x])

    def shift(slot, src, dst, step):
        return pltpu.make_async_remote_copy(
            src, dst, sh_send.at[slot], sh_recv.at[slot],
            device_id={"phase": lax.rem(phase + step, phase_count)}, device_id_type=MESH,
        )

    sub_iota = lax.broadcasted_iota(jnp.int32, (TILE, TILE), 0)
    lane_iota = lax.broadcasted_iota(jnp.int32, (TILE, TILE), 1)

    def build_want(b, carry):
        row = jnp.broadcast_to(idx[pl.ds(2 * blocks + b, 1), :], (TILE, TILE))
        col = jnp.transpose(row)
        for j in range(own_tiles):
            want_hot[rows_at(b, TILE), j * TILE:(j + 1) * TILE] = (col == lane_iota + j * TILE).astype(F32).astype(BF16)
        return carry

    lax.fori_loop(0, mirror_tiles, build_want, 0)

    def pick_rows(x, rows):
        def one(q, carry):
            picked = dot(want_hot[rows_at(q, TILE), :], rows[0:own_tiles].reshape(node_dev, features) if len(rows.shape) == 3 else rows[...])
            out_slab[x, pl.ds(pl.multiple_of(q * 16, 16), 16)] = to_slabs(picked)
            return carry

        lax.fori_loop(0, mirror_tiles, one, 0)

    pick_rows(0, ns)
    pl.semaphore_wait(barrier, dom_count - 1 + 2)
    start_exchange(0)
    pick_rows(1, nf)
    start_exchange(1)

    def build_edges(b, carry):
        for base_row, hot, hot_t in ((0, send_hot, send_hot_t), (blocks, recv_hot, recv_hot_t)):
            row = jnp.broadcast_to(jnp.bitwise_and(idx[pl.ds(base_row + b, 1), :], TILE - 1), (TILE, TILE))
            hot_t[b] = (row == sub_iota).astype(F32).astype(BF16)
            hot[b] = (jnp.transpose(row) == lane_iota).astype(F32).astype(BF16)
        return carry

    lax.fori_loop(0, blocks, build_edges, 0)

    for j in range(mirror_tiles):
        row = jnp.broadcast_to(idx[2 * blocks + j:2 * blocks + j + 1, :], (TILE, TILE))
        for i in range(own_tiles):
            want_hot_t[i * TILE:(i + 1) * TILE, j * TILE:(j + 1) * TILE] = (row == sub_iota + i * TILE).astype(F32).astype(BF16)

    table_s[0:own_tiles] = ns[...].reshape(own_tiles, TILE, features)
    table_f[0:own_tiles] = nf[...].reshape(own_tiles, TILE, features)

    def fetch(hot, b, table, first):
        return dot(hot[b], table[lax.div(sidx[first + b, 0], TILE)])

    def live_rows(i):
        at = lax.broadcasted_iota(jnp.int32, (CHUNK, features), 0) + i * CHUNK
        return jnp.where(at < cnt[0], 1.0, 0.0).astype(F32)

    def block_sum(hot_t, b, rows):
        high = rows.astype(BF16)
        low = (rows - high.astype(F32)).astype(BF16)
        return dot(jnp.concatenate([hot_t, hot_t], axis=1), jnp.concatenate([high, low], axis=0))

    def tile_total(k, first, count):
        total = jnp.zeros((TILE, features), F32)
        for b in range(count):
            tile = lax.div(idx[first + b:first + b + 1, 0:1], TILE)
            chosen = (tile == k).astype(F32)
            total = total + jnp.broadcast_to(chosen, (TILE, features)) * block_sums[b]
        return total

    def send_mirror_sums(x, first, count):
        def one(q, carry):
            total = tile_total(own_tiles + q, first, count)
            out_slab[x, pl.ds(pl.multiple_of(q * 16, 16), 16)] = to_slabs(total)
            return carry

        lax.fori_loop(0, mirror_tiles, one, 0)
        start_exchange(x)

    def own_sums(own, first, count):
        def one(k, carry):
            own[rows_at(k, TILE), :] = tile_total(k, first, count)
            return carry

        lax.fori_loop(0, own_tiles, one, 0)

    def edge_forward(edges, table, keep):
        def one(i, carry):
            rows = rows_at(i)
            from_send = jnp.concatenate(
                [fetch(send_hot, i * per_chunk + j, table, 0) for j in range(per_chunk)], axis=0
            ).astype(BF16)
            from_recv = jnp.concatenate(
                [fetch(recv_hot, i * per_chunk + j, table, blocks) for j in range(per_chunk)], axis=0
            ).astype(BF16)
            stacked = jnp.concatenate([edges[rows, :], from_send, from_recv], axis=1)
            pre = dot(stacked, w1[...]) + ev[0:1, :]
            hidden = jnp.maximum(pre, 0.0).astype(BF16)
            normed, inverse = layer_norm(dot(hidden, w2[...]) + ev[1:2, :])
            message = live_rows(i) * (normed * ev[2:3, :] + ev[3:4, :])
            if keep:
                sent_rows[rows, :] = from_send
                recv_rows[rows, :] = from_recv
                edge_pre[rows, :] = pre
                edge_hid[rows, :] = hidden
                edge_norm[rows, :] = normed
                edge_inv[rows, :] = inverse
            else:
                new_edges[rows, :] = (edges[rows, :].astype(F32) + message).astype(BF16)
            for j in range(per_chunk):
                b = i * per_chunk + j
                block_sums[b] = block_sum(recv_hot_t[b], b, message[j * TILE:(j + 1) * TILE, :])
            return carry

        lax.fori_loop(0, edge_chunks, one, 0)

    def node_forward(nodes, own, returned, keep):
        def one(i, carry):
            rows = rows_at(i)
            total = own[rows, :] + dot(want_hot_t[rows, :], returned)
            gathered = total.astype(BF16)
            stacked = jnp.concatenate([nodes[rows, :], gathered], axis=1)
            pre = dot(stacked, nw1[...]) + nv[0:1, :]
            hidden = jnp.maximum(pre, 0.0).astype(BF16)
            normed, inverse = layer_norm(dot(hidden, nw2[...]) + nv[1:2, :])
            if keep:
                agg_rows[rows, :] = gathered
                node_pre[rows, :] = pre
                node_hid[rows, :] = hidden
                node_norm[rows, :] = normed
                node_inv[rows, :] = inverse
            else:
                new_nodes[rows, :] = (
                    nodes[rows, :].astype(F32) + (normed * nv[2:3, :] + nv[3:4, :])
                ).astype(BF16)
            return carry

        lax.fori_loop(0, node_chunks, one, 0)

    table_s[own_tiles:] = wait_exchange(0).reshape(mirror_tiles, TILE, features)
    edge_forward(es, table_s, True)
    send_mirror_sums(2, blocks, blocks)
    own_sums(own_s, blocks, blocks)

    table_f[own_tiles:] = wait_exchange(1).reshape(mirror_tiles, TILE, features)
    edge_forward(ef, table_f, False)
    send_mirror_sums(3, blocks, blocks)
    shift(0, new_edges, o_ne, 1).start()
    own_sums(own_f, blocks, blocks)

    node_forward(ns, own_s, wait_exchange(2), True)

    def node_back(i, carry):
        s_first, s_pre, s_gain, s_shift = carry
        rows = rows_at(i)
        top = nc[rows, :].astype(F32)
        normed = node_norm[rows, :]
        pre_grad = norm_back(top * nv[2:3, :], normed, node_inv[rows, :]).astype(BF16)
        first = jnp.where(node_pre[rows, :] > 0.0, dot_nt(pre_grad, nw2[...]), 0.0).astype(BF16)
        node_pre_grad[rows, :] = pre_grad
        node_first_grad[rows, :] = first
        table_g[rows_at(i, per_chunk)] = dot_nt(first, nw1[features:, :]).astype(BF16).reshape(per_chunk, TILE, features)
        return (
            s_first + col_sum(first.astype(F32)),
            s_pre + col_sum(pre_grad.astype(F32)),
            s_gain + col_sum(top * normed),
            s_shift + col_sum(top),
        )

    zero_row = jnp.zeros((1, features), F32)
    sums = lax.fori_loop(0, node_chunks, node_back, (zero_row,) * 4)
    for j in range(4):
        vec[4 + j:5 + j, :] = sums[j]

    pick_rows(4, table_g)
    start_exchange(4)

    def start_a(which, grads, arrived, used):
        arrived[apos] = grads[apos]
        for k in range(1, GROUP):
            other, device = a_partner(k)
            pltpu.make_async_remote_copy(
                grads.at[other, pl.ds(0, used)], arrived.at[apos, pl.ds(0, used)],
                ra_s.at[which], ra_r.at[which], device_id={"dom": device}, device_id_type=MESH,
            ).start()

    def all_a(which, grads, arrived, used):
        part = pl.ds(0, GROUP - 1)
        return pltpu.make_async_remote_copy(
            grads.at[part, pl.ds(0, used)], arrived.at[part, pl.ds(0, used)],
            ra_s.at[which], ra_r.at[which], device_id={"dom": a_partner(1)[1]}, device_id_type=MESH,
        )

    def start_b(which, arrived):
        total = arrived[0].astype(F32)
        for k in range(1, GROUP):
            total = total + arrived[k].astype(F32)
        sb[which] = total.astype(BF16).reshape(Z_SIZE, 16, features)
        rb[which, zpos] = sb[which, zpos]
        for k in range(1, Z_SIZE):
            other, device = b_partner(k)
            pltpu.make_async_remote_copy(
                sb.at[which, other], rb.at[which, zpos], rb_s.at[which], rb_r.at[which],
                device_id={"dom": device}, device_id_type=MESH,
            ).start()

    def all_b(which):
        part = pl.ds(0, Z_SIZE - 1)
        return pltpu.make_async_remote_copy(
            sb.at[which, part], rb.at[which, part], rb_s.at[which], rb_r.at[which],
            device_id={"dom": b_partner(1)[1]}, device_id_type=MESH,
        )

    def start_gather_b(which):
        total = rb[which, 0].astype(F32)
        for k in range(1, Z_SIZE):
            total = total + rb[which, k].astype(F32)
        fb[which] = total.astype(BF16)
        ab[which, zpos] = fb[which]
        for k in range(1, Z_SIZE):
            other, device = b_partner(k)
            pltpu.make_async_remote_copy(
                fb.at[which], ab.at[which, zpos], gb_s.at[which], gb_r.at[which],
                device_id={"dom": device}, device_id_type=MESH,
            ).start()

    def all_gather_b(which):
        part = pl.ds(0, Z_SIZE - 1)
        return pltpu.make_async_remote_copy(
            ab.at[which, part], ab.at[which, part], gb_s.at[which], gb_r.at[which],
            device_id={"dom": b_partner(1)[1]}, device_id_type=MESH,
        )

    def start_gather_a(which, out):
        pltpu.make_async_copy(ab.at[which], out.at[apos], local_sem.at[which]).start()
        for k in range(1, GROUP):
            other, device = a_partner(k)
            pltpu.make_async_remote_copy(
                ab.at[which], out.at[apos], ga_s.at[which], ga_r.at[which],
                device_id={"dom": device}, device_id_type=MESH,
            ).start()

    def all_gather_a(which, out):
        part = pl.ds(0, GROUP - 1)
        return pltpu.make_async_remote_copy(
            out.at[part], out.at[part], ga_s.at[which], ga_r.at[which],
            device_id={"dom": a_partner(1)[1]}, device_id_type=MESH,
        )

    node_used = (3 * features) // GROUP

    def put_node_grads(first_row, grad):
        at = 0
        while at < grad.shape[0]:
            share, inner = divmod(first_row + at, node_used)
            size = min(node_used - inner, grad.shape[0] - at)
            g_node[share, inner:inner + size, :] = grad[at:at + size, :].astype(BF16)
            at += size

    for j in range(GROUP):
        g_node[j, node_used:, :] = jnp.zeros((TILE - node_used, features), BF16)
        ra_node[j, node_used:, :] = jnp.zeros((TILE - node_used, features), BF16)
    put_node_grads(0, dot_tn(ns[...], node_first_grad[...]))
    put_node_grads(features, dot_tn(agg_rows[...], node_first_grad[...]))
    put_node_grads(2 * features, dot_tn(node_hid[...], node_pre_grad[...]))
    start_a(0, g_node, ra_node, node_used)

    def node_base(i, carry):
        rows = rows_at(i)
        base[rows, :] = nc[rows, :].astype(F32) + dot_nt(node_first_grad[rows, :], nw1[:features, :])
        return carry

    lax.fori_loop(0, node_chunks, node_base, 0)

    node_forward(nf, own_f, wait_exchange(3), False)
    shift(1, new_nodes, o_nn, 1).start()

    all_a(0, g_node, ra_node, node_used).wait_recv()
    start_b(0, ra_node)

    table_g[own_tiles:] = wait_exchange(4).reshape(mirror_tiles, TILE, features)

    def edge_back(i, carry):
        s_first, s_pre, s_gain, s_shift = carry
        rows = rows_at(i)
        from_recv = jnp.concatenate(
            [fetch(recv_hot, i * per_chunk + j, table_g, blocks) for j in range(per_chunk)], axis=0
        )
        top = live_rows(i) * (ec[rows, :].astype(F32) + from_recv)
        normed = edge_norm[rows, :]
        pre_grad = norm_back(top * ev[2:3, :], normed, edge_inv[rows, :]).astype(BF16)
        first = jnp.where(edge_pre[rows, :] > 0.0, dot_nt(pre_grad, w2[...]), 0.0).astype(BF16)
        edge_pre_grad[rows, :] = pre_grad
        edge_first_grad[rows, :] = first
        to_send = dot_nt(first, w1[features:2 * features, :])
        to_recv = dot_nt(first, w1[2 * features:, :])
        for j in range(per_chunk):
            b = i * per_chunk + j
            block_sums[b] = block_sum(send_hot_t[b], b, to_send[j * TILE:(j + 1) * TILE, :])
            block_sums[blocks + b] = block_sum(recv_hot_t[b], b, to_recv[j * TILE:(j + 1) * TILE, :])
        return (
            s_first + col_sum(first.astype(F32)),
            s_pre + col_sum(pre_grad.astype(F32)),
            s_gain + col_sum(top * normed),
            s_shift + col_sum(top),
        )

    sums = lax.fori_loop(0, edge_chunks, edge_back, (zero_row,) * 4)
    for j in range(4):
        vec[j:j + 1, :] = sums[j]
    send_mirror_sums(5, 0, 2 * blocks)

    va[apos] = vec[...]
    for k in range(1, GROUP):
        other, device = a_partner(k)
        pltpu.make_async_remote_copy(
            vec, va.at[apos], v_s.at[0], v_r.at[0], device_id={"dom": device}, device_id_type=MESH
        ).start()

    def edge_out(i, carry):
        rows = rows_at(i)
        old_edges[rows, :] = (
            ec[rows, :].astype(F32) + dot_nt(edge_first_grad[rows, :], w1[:features, :])
        ).astype(BF16)
        return carry

    lax.fori_loop(0, edge_chunks, edge_out, 0)
    shift(2, old_edges, o_pe, phase_count - 1).start()

    for part, rows in enumerate((es, sent_rows, recv_rows)):
        grad = dot_tn(rows[...], edge_first_grad[...]).astype(BF16)
        g_edge[2 * part] = grad[:TILE, :]
        g_edge[2 * part + 1] = grad[TILE:, :]
    grad = dot_tn(edge_hid[...], edge_pre_grad[...]).astype(BF16)
    g_edge[6] = grad[:TILE, :]
    g_edge[7] = grad[TILE:, :]
    start_a(1, g_edge, ra_edge, TILE)

    own_sums(own_s, 0, 2 * blocks)
    all_b(0).wait_recv()
    start_gather_b(0)

    returned = wait_exchange(5)

    def node_out(i, carry):
        rows = rows_at(i)
        old_nodes[rows, :] = (
            base[rows, :] + own_s[rows, :] + dot(want_hot_t[rows, :], returned)
        ).astype(BF16)
        shift(3, old_nodes.at[rows, :], o_pn.at[rows, :], phase_count - 1).start()
        return carry

    lax.fori_loop(0, node_chunks, node_out, 0)

    all_a(1, g_edge, ra_edge, TILE).wait_recv()
    start_b(1, ra_edge)
    all_gather_b(0).wait_recv()
    start_gather_a(0, o_gn)

    group_part = pl.ds(0, GROUP - 1)
    first_all = pltpu.make_async_remote_copy(
        va.at[group_part], va.at[group_part], v_s.at[0], v_r.at[0],
        device_id={"dom": a_partner(1)[1]}, device_id_type=MESH,
    )
    first_all.wait_recv()
    first_all.wait_send()
    total = va[0]
    for k in range(1, GROUP):
        total = total + va[k]
    vec[...] = total
    vb[zpos] = total
    for k in range(1, Z_SIZE):
        other, device = b_partner(k)
        pltpu.make_async_remote_copy(
            vec, vb.at[zpos], v_s.at[1], v_r.at[1], device_id={"dom": device}, device_id_type=MESH
        ).start()

    all_b(1).wait_recv()
    start_gather_b(1)
    second_all = pltpu.make_async_remote_copy(
        vb.at[group_part], vb.at[group_part], v_s.at[1], v_r.at[1],
        device_id={"dom": b_partner(1)[1]}, device_id_type=MESH,
    )
    second_all.wait_recv()
    total = vb[0]
    for k in range(1, Z_SIZE):
        total = total + vb[k]
    o_gv[...] = total
    all_gather_b(1).wait_recv()
    start_gather_a(1, o_ge)

    for x in range(6):
        exchange_all(x).wait_send()
    all_a(0, g_node, ra_node, node_used).wait_send()
    all_a(1, g_edge, ra_edge, TILE).wait_send()
    second_all.wait_send()
    for which, out in ((0, o_gn), (1, o_ge)):
        all_b(which).wait_send()
        all_gather_b(which).wait_send()
        pltpu.make_async_copy(ab.at[which], out.at[apos], local_sem.at[which]).wait()
        all_gather_a(which, out).wait_send()
        all_gather_a(which, out).wait_recv()
    shift(0, new_edges, o_ne, 1).wait()
    shift(1, new_nodes, o_nn, 1).wait()
    shift(2, old_edges, o_pe, phase_count - 1).wait()
    shift(3, old_nodes, o_pn, phase_count - 1).wait()


def tick(dom_count, phase_count, *arrays):
    edge_dev, features = arrays[0].shape
    node_dev = arrays[1].shape[0]
    blocks = edge_dev // TILE
    slots = node_dev + dom_count * 8
    vmem = lambda shape, kind=BF16: pltpu.VMEM(shape, kind)
    sem = lambda count: pltpu.SemaphoreType.DMA((count,))
    scratch = (
        [vmem((blocks, TILE, TILE))] * 4
        + [vmem((dom_count * 8, node_dev)), vmem((node_dev, dom_count * 8))]
        + [vmem((slots // TILE, TILE, features))] * 3
        + [vmem((6, dom_count, 16, 128))] * 2
        + [vmem((edge_dev, features))] * 2
        + [vmem((edge_dev, features), F32), vmem((edge_dev, features)), vmem((edge_dev, features), F32), vmem((edge_dev, 1), F32)]
        + [vmem((edge_dev, features))] * 2
        + [vmem((node_dev, features), F32), vmem((node_dev, features)), vmem((node_dev, features), F32), vmem((node_dev, 1), F32)]
        + [vmem((node_dev, features))] * 3
        + [vmem((2 * blocks, TILE, features), F32)]
        + [vmem((node_dev, features), F32)] * 3
        + [vmem((edge_dev, features)), vmem((node_dev, features))] * 2
        + [vmem((GROUP, TILE, features))] * 4
        + [vmem((2, Z_SIZE, 16, features))] * 2
        + [vmem((2, 16, features)), vmem((2, Z_SIZE, 16, features))]
        + [vmem((GROUP, 8, features), F32), vmem((Z_SIZE, 8, features), F32), vmem((8, features), F32)]
        + [sem(6), sem(6), sem(4), sem(4)]
        + [sem(2)] * 11
    )
    in_vmem = pl.BlockSpec(memory_space=pltpu.VMEM)
    in_smem = pl.BlockSpec(memory_space=pltpu.SMEM)
    anywhere = pl.BlockSpec(memory_space=pl.ANY)
    out_shape = (
        jax.ShapeDtypeStruct((edge_dev, features), BF16),
        jax.ShapeDtypeStruct((node_dev, features), BF16),
        jax.ShapeDtypeStruct((edge_dev, features), BF16),
        jax.ShapeDtypeStruct((node_dev, features), BF16),
        jax.ShapeDtypeStruct((GROUP, Z_SIZE, 16, features), BF16),
        jax.ShapeDtypeStruct((GROUP, Z_SIZE, 16, features), BF16),
        jax.ShapeDtypeStruct((8, features), F32),
    )

    def kernel(*refs):
        tick_kernel(dom_count, phase_count, *refs)

    return pl.pallas_call(
        kernel,
        out_shape=out_shape,
        in_specs=[in_vmem] * 13 + [in_smem] * 2,
        out_specs=[anywhere] * 6 + [in_vmem],
        scratch_shapes=scratch,
        name="tick",
        compiler_params=pltpu.CompilerParams(
            collective_id=0, has_side_effects=True, vmem_limit_bytes=48 * 2**20
        ),
    )(*arrays)


def on_device(
    edges_fwd, nodes_fwd, edges_stash, nodes_stash, edge_cot, node_cot,
    edge_w1, edge_w2, edge_vectors, node_w1, node_w2, node_vectors,
    edge_nodes, mirror_rows, edge_count,
):
    dom_count = lax.axis_size("dom")
    phase_count = lax.axis_size("phase")
    features = edges_fwd.shape[2]
    rows = jnp.concatenate(
        [edge_nodes.reshape(-1, TILE), mirror_rows.reshape(-1, TILE)], axis=0
    ).astype(jnp.int32)
    ne, nn, pe, pn, ge, gn, gv = tick(
        dom_count, phase_count,
        edges_fwd[0], nodes_fwd[0], edges_stash[0], nodes_stash[0], edge_cot[0], node_cot[0],
        edge_w1[0], edge_w2[0], edge_vectors[0], node_w1[0], node_w2[0], node_vectors[0],
        rows, rows, edge_count,
    )
    ge = ge.reshape(-1, features)
    node_used = (3 * features) // GROUP
    gn = gn.reshape(GROUP, TILE, features)[:, :node_used].reshape(-1, features)
    return (
        ne[None], nn[None], pe[None], pn[None],
        ge[: 3 * features].astype(F32)[None],
        ge[3 * features :].astype(F32)[None],
        gv[:4][None],
        gn[: 2 * features].astype(F32)[None],
        gn[2 * features :].astype(F32)[None],
        gv[4:][None],
    )


def solution(mesh):
    rows = P("phase", "dom", None)
    whole = P("phase", None, None)
    in_specs = (rows,) * 6 + (whole,) * 6 + (P(None, "dom"), P("dom", None, None), P("dom"))
    out_specs = (rows,) * 4 + (whole,) * 6
    return jax.shard_map(
        on_device, mesh=mesh, in_specs=in_specs, out_specs=out_specs, check_vma=False
    )
```

profile of v0, /device:TPU:1, one launch (start us, length us, event | category | flops | bytes accessed | tf_op | source)
XLA Modules:
  0.0 103.2 jit_solution(10954160679293121278)
XLA Ops:
  0.6 0.0 copy-start.12
  0.7 0.7 copy-done.12
  1.3 0.1 copy.26
  1.4 0.0 copy-start.11
  1.4 0.1 reshape.60
  1.5 0.6 copy-done.11
  2.1 0.0 copy-start.9
  2.1 0.0 copy-start.10
  2.8 0.0 copy-done.9
  2.8 0.0 copy-done.10
  2.8 0.0 copy-start
  2.8 1.0 %copy-done = bf16[1,1024,256]{2,1,0:T(8,128)(2,1)S(1)} copy-done((bf16[1,1024,256]{2,1,0:T(8,128)(2,1)S(1)}, bf16[1,1024,256]{2,1,0:T(8,128)(2,1)}, u32[]{:S(2)}) %copy-start) | copy-done | bytes 524312
  3.9 1.0 %copy-done.1 = bf16[1,1024,256]{2,1,0:T(8,128)(2,1)S(1)} copy-done((bf16[1,1024,256]{2,1,0:T(8,128)(2,1)S(1)}, bf16[1,1024,256]{2,1,0:T(8,128)(2,1)}, u32[]{:S(2)}) %copy-start.1) | copy-done | bytes 524312
  4.9 0.0 copy-start.2
  4.9 1.0 copy-done.2
  5.9 0.0 copy-start.3
  5.9 1.0 copy-done.3
  6.9 1.0 copy-done.4
  7.9 1.0 copy-done.5
  8.9 0.9 copy-done.6
  9.8 0.9 copy-done.7
  10.8 0.9 copy-done.8
  11.7 84.6 %tick.1 = (bf16[768,256]{1,0:T(8,128)(2,1)S(1)}, bf16[1024,256]{1,0:T(8,128)(2,1)S(1)}, bf16[768,256]{1,0:T(8,128)(2,1)S(1)}, bf16[1024,256]{1,0:T(8,128)(2,1)S(...) custom-call(bf16[768,256]{1,0:T(8,128)(2,1)S(1)} %bitcast.42, ...), custom_call_target="tpu_custom_call" | custom-call | tf_op jit(solution)/shard_map/tick/pallas_call | solution.py:590
  96.3 0.9 convert.4
  97.2 0.7 convert.5
  97.9 0.6 slice_bitcast_fusion.2
  98.6 0.8 fusion
  99.4 0.7 fusion.1
  100.1 0.7 copy.32
  100.9 0.8 copy.33
  101.7 0.7 copy.34
  102.4 0.8 copy.35
  (11 shorter events, 0.1 us)
Async XLA Ops:
  0.6 0.7 copy-start.12
  1.4 0.7 copy-start.11
  2.1 0.7 copy-start.9
  2.1 0.7 copy-start.10
  2.8 1.0 %copy-start = (bf16[1,1024,256]{2,1,0:T(8,128)(2,1)S(1)}, bf16[1,1024,256]{2,1,0:T(8,128)(2,1)}, u32[]{:S(2)}) copy-start(bf16[1,1024,256]{2,1,0:T(8,128)(2,1)} %param.16) | copy-start | bytes 1572868
  3.9 1.0 %copy-start.1 = (bf16[1,1024,256]{2,1,0:T(8,128)(2,1)S(1)}, bf16[1,1024,256]{2,1,0:T(8,128)(2,1)}, u32[]{:S(2)}) copy-start(bf16[1,1024,256]{2,1,0:T(8,128)(2,1)} %param.18) | copy-start | bytes 1572868
  4.9 1.0 copy-start.2
  5.9 1.0 copy-start.3
  6.9 1.0 copy-start.4
  7.9 1.0 copy-start.5
  8.9 0.9 copy-start.6
  9.8 0.9 copy-start.7
  10.7 0.9 copy-start.8
where the time goes:
time: 104 us; the launch traced here: 103 us
  Pallas kernels  84.6 us (81%)
  local copies, waits for them, and re-layouts  14 us (13%)
  other arithmetic  3.22 us (3%)
  between operations  1.37 us (1%)
    pallas_call x1, Pallas kernels, tick(): pl.pallas_call(kernel, out_shape=out_shape, in_specs=[in_vmem] * 13 + [in...  84.6 us
    unnamed x31, local copies, waits for them, and re-layouts  13.3 us

commit v1 on v0

--- a/solution.py
+++ b/solution.py
@@ -12,7 +12,10 @@
 F32 = jnp.float32
 BF16 = jnp.bfloat16
 MESH = pl.DeviceIdType.MESH
-CHUNK = 256
+EDGE_CHUNK = 768
+NODE_CHUNK = 1024
+UNROLL = False
+VMEM_BYTES = 63 * 2**20
 
 
 def dot(a, b, contract=((1,), (0,))):
@@ -60,15 +63,16 @@
     return jnp.sum(rows, axis=0, keepdims=True)
 
 
-def rows_at(i, size=CHUNK):
+def rows_at(i, size):
     return pl.ds(pl.multiple_of(i * size, size), size)
 
 
 def tick_kernel(
     dom_count,
     phase_count,
-    ef, nf, es, ns, ec, nc, w1, w2, ev, nw1, nw2, nv, idx, sidx, cnt,
+    h_ef, h_nf, h_es, h_ns, h_ec, h_nc, h_w1, h_w2, h_ev, h_nw1, h_nw2, h_nv, ends, mirror, s_ends, cnt,
     o_ne, o_nn, o_pe, o_pn, o_ge, o_gn, o_gv,
+    ef, nf, es, ns, ec, nc, w1, w2, ev, nw1, nw2, nv, want_row,
     send_hot, send_hot_t, recv_hot, recv_hot_t, want_hot, want_hot_t,
     table_s, table_f, table_g, out_slab, in_slab,
     sent_rows, recv_rows, edge_pre, edge_hid, edge_norm, edge_inv, edge_pre_grad, edge_first_grad,
@@ -76,7 +80,7 @@
     block_sums, own_s, own_f, base,
     new_edges, new_nodes, old_edges, old_nodes,
     g_edge, g_node, ra_edge, ra_node, sb, rb, fb, ab, va, vb, vec,
-    x_send, x_recv, sh_send, sh_recv, ra_s, ra_r, rb_s, rb_r, gb_s, gb_r, ga_s, ga_r, v_s, v_r, local_sem,
+    x_send, x_recv, sh_send, sh_recv, ra_s, ra_r, rb_s, rb_r, gb_s, gb_r, ga_s, ga_r, v_s, v_r, local_sem, in_sem,
 ):
     me = lax.axis_index("dom")
     phase = lax.axis_index("phase")
@@ -88,9 +92,9 @@
     blocks = edge_dev // TILE
     own_tiles = node_dev // TILE
     mirror_tiles = (dom_count * 8) // TILE
-    node_chunks = node_dev // CHUNK
-    edge_chunks = edge_dev // CHUNK
-    per_chunk = CHUNK // TILE
+    node_chunks = node_dev // NODE_CHUNK
+    edge_chunks = edge_dev // EDGE_CHUNK
+    per_chunk = EDGE_CHUNK // TILE
 
     def a_partner(k):
         other = lax.rem(apos + k, GROUP)
@@ -99,6 +103,17 @@
     def b_partner(k):
         other = lax.rem(zpos + k, Z_SIZE)
         return other, me + 2 * (other - zpos)
+
+    operands = [
+        (h_ns, ns), (h_nf, nf), (h_es, es), (h_w1, w1), (h_w2, w2), (h_ev, ev), (h_ef, ef),
+        (h_nw1, nw1), (h_nw2, nw2), (h_nv, nv), (h_nc, nc), (h_ec, ec),
+    ]
+
+    def operand(n):
+        return pltpu.make_async_copy(operands[n][0], operands[n][1], in_sem.at[n])
+
+    for n in range(len(operands)):
+        operand(n).start()
 
     barrier = pltpu.get_barrier_semaphore()
 
@@ -146,11 +161,23 @@
     sub_iota = lax.broadcasted_iota(jnp.int32, (TILE, TILE), 0)
     lane_iota = lax.broadcasted_iota(jnp.int32, (TILE, TILE), 1)
 
+    slab_iota = lax.broadcasted_iota(jnp.int32, (TILE, dom_count), 0)
+    dom_iota = lax.broadcasted_iota(jnp.int32, (TILE, dom_count), 1)
+    in_slab_iota = lax.broadcasted_iota(jnp.int32, (TILE, 8), 0)
+    cap_iota = lax.broadcasted_iota(jnp.int32, (TILE, 8), 1)
+    lane_float = lane_iota.astype(F32)
+    sub_float = sub_iota.astype(F32)
+    mirror_high = lax.div(mirror[...], 8).astype(F32).astype(BF16)
+    mirror_low = lax.rem(mirror[...], 8).astype(F32).astype(BF16)
+
     def build_want(b, carry):
-        row = jnp.broadcast_to(idx[pl.ds(2 * blocks + b, 1), :], (TILE, TILE))
-        col = jnp.transpose(row)
+        owner = (dom_iota == b * 16 + lax.div(slab_iota, 8)).astype(F32).astype(BF16)
+        named = dot_nt(owner, mirror_high) * 8.0 + dot_nt(owner, mirror_low)
+        named = jnp.where(cap_iota == lax.rem(in_slab_iota, 8), named, 0.0)
+        col = jnp.broadcast_to(jnp.sum(named, axis=1, keepdims=True), (TILE, TILE))
+        want_row[b] = jnp.transpose(col)[:8]
         for j in range(own_tiles):
-            want_hot[rows_at(b, TILE), j * TILE:(j + 1) * TILE] = (col == lane_iota + j * TILE).astype(F32).astype(BF16)
+            want_hot[rows_at(b, TILE), j * TILE:(j + 1) * TILE] = (col == lane_float + float(j * TILE)).astype(F32).astype(BF16)
         return carry
 
     lax.fori_loop(0, mirror_tiles, build_want, 0)
@@ -163,15 +190,17 @@
 
         lax.fori_loop(0, mirror_tiles, one, 0)
 
+    operand(0).wait()
     pick_rows(0, ns)
     pl.semaphore_wait(barrier, dom_count - 1 + 2)
     start_exchange(0)
+    operand(1).wait()
     pick_rows(1, nf)
     start_exchange(1)
 
     def build_edges(b, carry):
-        for base_row, hot, hot_t in ((0, send_hot, send_hot_t), (blocks, recv_hot, recv_hot_t)):
-            row = jnp.broadcast_to(jnp.bitwise_and(idx[pl.ds(base_row + b, 1), :], TILE - 1), (TILE, TILE))
+        for end, hot, hot_t in ((0, send_hot, send_hot_t), (1, recv_hot, recv_hot_t)):
+            row = jnp.broadcast_to(jnp.bitwise_and(ends[end:end + 1, rows_at(b, TILE)], TILE - 1), (TILE, TILE))
             hot_t[b] = (row == sub_iota).astype(F32).astype(BF16)
             hot[b] = (jnp.transpose(row) == lane_iota).astype(F32).astype(BF16)
         return carry
@@ -179,18 +208,18 @@
     lax.fori_loop(0, blocks, build_edges, 0)
 
     for j in range(mirror_tiles):
-        row = jnp.broadcast_to(idx[2 * blocks + j:2 * blocks + j + 1, :], (TILE, TILE))
+        row = jnp.broadcast_to(want_row[j, 0:1, :], (TILE, TILE))
         for i in range(own_tiles):
-            want_hot_t[i * TILE:(i + 1) * TILE, j * TILE:(j + 1) * TILE] = (row == sub_iota + i * TILE).astype(F32).astype(BF16)
+            want_hot_t[i * TILE:(i + 1) * TILE, j * TILE:(j + 1) * TILE] = (row == sub_float + float(i * TILE)).astype(F32).astype(BF16)
 
     table_s[0:own_tiles] = ns[...].reshape(own_tiles, TILE, features)
     table_f[0:own_tiles] = nf[...].reshape(own_tiles, TILE, features)
 
-    def fetch(hot, b, table, first):
-        return dot(hot[b], table[lax.div(sidx[first + b, 0], TILE)])
+    def fetch(hot, b, table, end):
+        return dot(hot[b], table[lax.div(s_ends[end, b * TILE], TILE)])
 
     def live_rows(i):
-        at = lax.broadcasted_iota(jnp.int32, (CHUNK, features), 0) + i * CHUNK
+        at = lax.broadcasted_iota(jnp.int32, (EDGE_CHUNK, features), 0) + i * EDGE_CHUNK
         return jnp.where(at < cnt[0], 1.0, 0.0).astype(F32)
 
     def block_sum(hot_t, b, rows):
@@ -201,7 +230,8 @@
     def tile_total(k, first, count):
         total = jnp.zeros((TILE, features), F32)
         for b in range(count):
-            tile = lax.div(idx[first + b:first + b + 1, 0:1], TILE)
+            end, block = divmod(first + b, blocks)
+            tile = lax.div(ends[end:end + 1, block * TILE:block * TILE + 1], TILE)
             chosen = (tile == k).astype(F32)
             total = total + jnp.broadcast_to(chosen, (TILE, features)) * block_sums[b]
         return total
@@ -224,12 +254,12 @@
 
     def edge_forward(edges, table, keep):
         def one(i, carry):
-            rows = rows_at(i)
+            rows = rows_at(i, EDGE_CHUNK)
             from_send = jnp.concatenate(
                 [fetch(send_hot, i * per_chunk + j, table, 0) for j in range(per_chunk)], axis=0
             ).astype(BF16)
             from_recv = jnp.concatenate(
-                [fetch(recv_hot, i * per_chunk + j, table, blocks) for j in range(per_chunk)], axis=0
+                [fetch(recv_hot, i * per_chunk + j, table, 1) for j in range(per_chunk)], axis=0
             ).astype(BF16)
             stacked = jnp.concatenate([edges[rows, :], from_send, from_recv], axis=1)
             pre = dot(stacked, w1[...]) + ev[0:1, :]
@@ -250,11 +280,11 @@
                 block_sums[b] = block_sum(recv_hot_t[b], b, message[j * TILE:(j + 1) * TILE, :])
             return carry
 
-        lax.fori_loop(0, edge_chunks, one, 0)
+        lax.fori_loop(0, edge_chunks, one, 0, unroll=UNROLL)
 
     def node_forward(nodes, own, returned, keep):
         def one(i, carry):
-            rows = rows_at(i)
+            rows = rows_at(i, NODE_CHUNK)
             total = own[rows, :] + dot(want_hot_t[rows, :], returned)
             gathered = total.astype(BF16)
             stacked = jnp.concatenate([nodes[rows, :], gathered], axis=1)
@@ -273,31 +303,36 @@
                 ).astype(BF16)
             return carry
 
-        lax.fori_loop(0, node_chunks, one, 0)
-
+        lax.fori_loop(0, node_chunks, one, 0, unroll=UNROLL)
+
+    for n in (2, 3, 4, 5):
+        operand(n).wait()
     table_s[own_tiles:] = wait_exchange(0).reshape(mirror_tiles, TILE, features)
     edge_forward(es, table_s, True)
     send_mirror_sums(2, blocks, blocks)
     own_sums(own_s, blocks, blocks)
 
+    operand(6).wait()
     table_f[own_tiles:] = wait_exchange(1).reshape(mirror_tiles, TILE, features)
     edge_forward(ef, table_f, False)
     send_mirror_sums(3, blocks, blocks)
     shift(0, new_edges, o_ne, 1).start()
     own_sums(own_f, blocks, blocks)
 
+    for n in (7, 8, 9, 10):
+        operand(n).wait()
     node_forward(ns, own_s, wait_exchange(2), True)
 
     def node_back(i, carry):
         s_first, s_pre, s_gain, s_shift = carry
-        rows = rows_at(i)
+        rows = rows_at(i, NODE_CHUNK)
         top = nc[rows, :].astype(F32)
         normed = node_norm[rows, :]
         pre_grad = norm_back(top * nv[2:3, :], normed, node_inv[rows, :]).astype(BF16)
         first = jnp.where(node_pre[rows, :] > 0.0, dot_nt(pre_grad, nw2[...]), 0.0).astype(BF16)
         node_pre_grad[rows, :] = pre_grad
         node_first_grad[rows, :] = first
-        table_g[rows_at(i, per_chunk)] = dot_nt(first, nw1[features:, :]).astype(BF16).reshape(per_chunk, TILE, features)
+        table_g[rows_at(i, NODE_CHUNK // TILE)] = dot_nt(first, nw1[features:, :]).astype(BF16).reshape(NODE_CHUNK // TILE, TILE, features)
         return (
             s_first + col_sum(first.astype(F32)),
             s_pre + col_sum(pre_grad.astype(F32)),
@@ -306,7 +341,7 @@
         )
 
     zero_row = jnp.zeros((1, features), F32)
-    sums = lax.fori_loop(0, node_chunks, node_back, (zero_row,) * 4)
+    sums = lax.fori_loop(0, node_chunks, node_back, (zero_row,) * 4, unroll=UNROLL)
     for j in range(4):
         vec[4 + j:5 + j, :] = sums[j]
 
@@ -404,11 +439,11 @@
     start_a(0, g_node, ra_node, node_used)
 
     def node_base(i, carry):
-        rows = rows_at(i)
+        rows = rows_at(i, NODE_CHUNK)
         base[rows, :] = nc[rows, :].astype(F32) + dot_nt(node_first_grad[rows, :], nw1[:features, :])
         return carry
 
-    lax.fori_loop(0, node_chunks, node_base, 0)
+    lax.fori_loop(0, node_chunks, node_base, 0, unroll=UNROLL)
 
     node_forward(nf, own_f, wait_exchange(3), False)
     shift(1, new_nodes, o_nn, 1).start()
@@ -416,13 +451,14 @@
     all_a(0, g_node, ra_node, node_used).wait_recv()
     start_b(0, ra_node)
 
+    operand(11).wait()
     table_g[own_tiles:] = wait_exchange(4).reshape(mirror_tiles, TILE, features)
 
     def edge_back(i, carry):
         s_first, s_pre, s_gain, s_shift = carry
-        rows = rows_at(i)
+        rows = rows_at(i, EDGE_CHUNK)
         from_recv = jnp.concatenate(
-            [fetch(recv_hot, i * per_chunk + j, table_g, blocks) for j in range(per_chunk)], axis=0
+            [fetch(recv_hot, i * per_chunk + j, table_g, 1) for j in range(per_chunk)], axis=0
         )
         top = live_rows(i) * (ec[rows, :].astype(F32) + from_recv)
         normed = edge_norm[rows, :]
@@ -443,7 +479,7 @@
             s_shift + col_sum(top),
         )
 
-    sums = lax.fori_loop(0, edge_chunks, edge_back, (zero_row,) * 4)
+    sums = lax.fori_loop(0, edge_chunks, edge_back, (zero_row,) * 4, unroll=UNROLL)
     for j in range(4):
         vec[j:j + 1, :] = sums[j]
     send_mirror_sums(5, 0, 2 * blocks)
@@ -454,16 +490,6 @@
         pltpu.make_async_remote_copy(
             vec, va.at[apos], v_s.at[0], v_r.at[0], device_id={"dom": device}, device_id_type=MESH
         ).start()
-
-    def edge_out(i, carry):
-        rows = rows_at(i)
-        old_edges[rows, :] = (
-            ec[rows, :].astype(F32) + dot_nt(edge_first_grad[rows, :], w1[:features, :])
-        ).astype(BF16)
-        return carry
-
-    lax.fori_loop(0, edge_chunks, edge_out, 0)
-    shift(2, old_edges, o_pe, phase_count - 1).start()
 
     for part, rows in enumerate((es, sent_rows, recv_rows)):
         grad = dot_tn(rows[...], edge_first_grad[...]).astype(BF16)
@@ -474,24 +500,36 @@
     g_edge[7] = grad[TILE:, :]
     start_a(1, g_edge, ra_edge, TILE)
 
+    def edge_out(i, carry):
+        rows = rows_at(i, EDGE_CHUNK)
+        old_edges[rows, :] = (
+            ec[rows, :].astype(F32) + dot_nt(edge_first_grad[rows, :], w1[:features, :])
+        ).astype(BF16)
+        return carry
+
+    lax.fori_loop(0, edge_chunks, edge_out, 0, unroll=UNROLL)
+    shift(2, old_edges, o_pe, phase_count - 1).start()
+
     own_sums(own_s, 0, 2 * blocks)
     all_b(0).wait_recv()
     start_gather_b(0)
+    all_a(1, g_edge, ra_edge, TILE).wait_recv()
+    start_b(1, ra_edge)
 
     returned = wait_exchange(5)
 
     def node_out(i, carry):
-        rows = rows_at(i)
+        rows = rows_at(i, NODE_CHUNK)
         old_nodes[rows, :] = (
             base[rows, :] + own_s[rows, :] + dot(want_hot_t[rows, :], returned)
         ).astype(BF16)
         shift(3, old_nodes.at[rows, :], o_pn.at[rows, :], phase_count - 1).start()
         return carry
 
-    lax.fori_loop(0, node_chunks, node_out, 0)
-
-    all_a(1, g_edge, ra_edge, TILE).wait_recv()
-    start_b(1, ra_edge)
+    lax.fori_loop(0, node_chunks, node_out, 0, unroll=UNROLL)
+
+    all_b(1).wait_recv()
+    start_gather_b(1)
     all_gather_b(0).wait_recv()
     start_gather_a(0, o_gn)
 
@@ -513,8 +551,8 @@
             vec, vb.at[zpos], v_s.at[1], v_r.at[1], device_id={"dom": device}, device_id_type=MESH
         ).start()
 
-    all_b(1).wait_recv()
-    start_gather_b(1)
+    all_gather_b(1).wait_recv()
+    start_gather_a(1, o_ge)
     second_all = pltpu.make_async_remote_copy(
         vb.at[group_part], vb.at[group_part], v_s.at[1], v_r.at[1],
         device_id={"dom": b_partner(1)[1]}, device_id_type=MESH,
@@ -524,8 +562,6 @@
     for k in range(1, Z_SIZE):
         total = total + vb[k]
     o_gv[...] = total
-    all_gather_b(1).wait_recv()
-    start_gather_a(1, o_ge)
 
     for x in range(6):
         exchange_all(x).wait_send()
@@ -551,8 +587,11 @@
     slots = node_dev + dom_count * 8
     vmem = lambda shape, kind=BF16: pltpu.VMEM(shape, kind)
     sem = lambda count: pltpu.SemaphoreType.DMA((count,))
+    mirror_tiles = dom_count * 8 // TILE
     scratch = (
-        [vmem((blocks, TILE, TILE))] * 4
+        [vmem(a.shape, a.dtype) for a in arrays[:12]]
+        + [vmem((mirror_tiles, 8, TILE), F32)]
+        + [vmem((blocks, TILE, TILE))] * 4
         + [vmem((dom_count * 8, node_dev)), vmem((node_dev, dom_count * 8))]
         + [vmem((slots // TILE, TILE, features))] * 3
         + [vmem((6, dom_count, 16, 128))] * 2
@@ -570,7 +609,9 @@
         + [vmem((GROUP, 8, features), F32), vmem((Z_SIZE, 8, features), F32), vmem((8, features), F32)]
         + [sem(6), sem(6), sem(4), sem(4)]
         + [sem(2)] * 11
+        + [sem(12)]
     )
+    in_hbm = pl.BlockSpec(memory_space=pltpu.HBM)
     in_vmem = pl.BlockSpec(memory_space=pltpu.VMEM)
     in_smem = pl.BlockSpec(memory_space=pltpu.SMEM)
     anywhere = pl.BlockSpec(memory_space=pl.ANY)
@@ -590,14 +631,77 @@
     return pl.pallas_call(
         kernel,
         out_shape=out_shape,
-        in_specs=[in_vmem] * 13 + [in_smem] * 2,
+        in_specs=[in_hbm] * 12 + [in_vmem] * 2 + [in_smem] * 2,
         out_specs=[anywhere] * 6 + [in_vmem],
         scratch_shapes=scratch,
         name="tick",
         compiler_params=pltpu.CompilerParams(
-            collective_id=0, has_side_effects=True, vmem_limit_bytes=48 * 2**20
+            collective_id=0, has_side_effects=True, vmem_limit_bytes=VMEM_BYTES
         ),
     )(*arrays)
+
+
+def hand_over_kernel(
+    ne, nn, pe, pn, ge, gn, gv,
+    o_ne, o_nn, o_pe, o_pn, o_ew1, o_ew2, o_ev, o_nw1, o_nw2, o_nv,
+    ew1, ew2, nw1, nw2, v_ne, v_nn, v_pe, v_pn, v_ge, v_gn, v_gv, in_sems, sems,
+):
+    features = gv.shape[1]
+    arriving = [(gn, v_gn), (ge, v_ge), (gv, v_gv), (ne, v_ne), (nn, v_nn), (pe, v_pe), (pn, v_pn)]
+    arriving = [pltpu.make_async_copy(src, dst, in_sems.at[n]) for n, (src, dst) in enumerate(arriving)]
+    copies = [(v_ne, o_ne.at[0]), (v_nn, o_nn.at[0]), (v_pe, o_pe.at[0]), (v_pn, o_pn.at[0])]
+    copies += [(v_gv.at[pl.ds(0, 4)], o_ev.at[0]), (v_gv.at[pl.ds(4, 4)], o_nv.at[0])]
+    copies += [(ew1, o_ew1.at[0]), (ew2, o_ew2.at[0]), (nw1, o_nw1.at[0]), (nw2, o_nw2.at[0])]
+    copies = [pltpu.make_async_copy(src, dst, sems.at[n]) for n, (src, dst) in enumerate(copies)]
+    for copy in arriving:
+        copy.start()
+    arriving[0].wait()
+    used = (3 * features) // GROUP
+    cut = 2 * features
+    for share in range(GROUP):
+        rows = v_gn[share, 0:used // 16].reshape(used, features).astype(F32)
+        first = share * used
+        inner = min(max(cut - first, 0), used)
+        if inner > 0:
+            nw1[first:first + inner, :] = rows[:inner]
+        if inner < used:
+            nw2[first + inner - cut:first + used - cut, :] = rows[inner:]
+    copies[8].start()
+    copies[9].start()
+    arriving[1].wait()
+    ew1[...] = v_ge[0:6].reshape(3 * features, features).astype(F32)
+    copies[6].start()
+    ew2[...] = v_ge[6:8].reshape(features, features).astype(F32)
+    copies[7].start()
+    arriving[2].wait()
+    copies[4].start()
+    copies[5].start()
+    for n in range(4):
+        arriving[3 + n].wait()
+        copies[n].start()
+    for copy in copies:
+        copy.wait()
+
+
+def hand_over(ne, nn, pe, pn, ge, gn, gv):
+    features = gv.shape[1]
+    shape = lambda rows, kind: jax.ShapeDtypeStruct((1, rows, features), kind)
+    out_shape = tuple(shape(a.shape[0], BF16) for a in (ne, nn, pe, pn)) + (
+        shape(3 * features, F32), shape(features, F32), shape(4, F32),
+        shape(2 * features, F32), shape(features, F32), shape(4, F32),
+    )
+    grads = [pltpu.VMEM((n * features, features), F32) for n in (3, 1, 2, 1)]
+    held = [pltpu.VMEM(a.shape, a.dtype) for a in (ne, nn, pe, pn, ge, gn, gv)]
+    in_hbm = pl.BlockSpec(memory_space=pltpu.HBM)
+    return pl.pallas_call(
+        hand_over_kernel,
+        out_shape=out_shape,
+        in_specs=[in_hbm] * 7,
+        out_specs=[in_hbm] * 10,
+        scratch_shapes=grads + held + [pltpu.SemaphoreType.DMA((7,)), pltpu.SemaphoreType.DMA((10,))],
+        name="hand_over",
+        compiler_params=pltpu.CompilerParams(vmem_limit_bytes=VMEM_BYTES),
+    )(ne, nn, pe, pn, ge, gn, gv)
 
 
 def on_device(
@@ -608,27 +712,13 @@
     dom_count = lax.axis_size("dom")
     phase_count = lax.axis_size("phase")
     features = edges_fwd.shape[2]
-    rows = jnp.concatenate(
-        [edge_nodes.reshape(-1, TILE), mirror_rows.reshape(-1, TILE)], axis=0
-    ).astype(jnp.int32)
     ne, nn, pe, pn, ge, gn, gv = tick(
         dom_count, phase_count,
         edges_fwd[0], nodes_fwd[0], edges_stash[0], nodes_stash[0], edge_cot[0], node_cot[0],
         edge_w1[0], edge_w2[0], edge_vectors[0], node_w1[0], node_w2[0], node_vectors[0],
-        rows, rows, edge_count,
+        edge_nodes, mirror_rows[0].T, edge_nodes, edge_count,
     )
-    ge = ge.reshape(-1, features)
-    node_used = (3 * features) // GROUP
-    gn = gn.reshape(GROUP, TILE, features)[:, :node_used].reshape(-1, features)
-    return (
-        ne[None], nn[None], pe[None], pn[None],
-        ge[: 3 * features].astype(F32)[None],
-        ge[3 * features :].astype(F32)[None],
-        gv[:4][None],
-        gn[: 2 * features].astype(F32)[None],
-        gn[2 * features :].astype(F32)[None],
-        gv[4:][None],
-    )
+    return hand_over(ne, nn, pe, pn, ge, gn, gv)
 
 
 def solution(mesh):

time: 104 us -> 85.7 us (0.82)
  local copies, waits for them, and re-layouts: 14 us -> 0 us
  other arithmetic: 3.22 us -> 0 us
    unnamed x31 -> x0, local copies, waits for them, and re-layouts: 13.3 us -> none
    convert_element_type x2 -> x0, other arithmetic: 1.66 us -> none  [the longest x1 0.94 us: on_device(): ge[:3 * features].astype(F32)[None]]
    broadcast_in_dim x2 -> x0, other arithmetic: 1.55 us -> none  [the longest x1 0.83 us: on_device(): gn[:2 * features].astype(F32)[None]]
    pallas_call x1 -> x2, Pallas kernels: 84.6 us -> 84.2 us  [the longest x1 81.2 us: tick(): pl.pallas_call(kernel, out_shape=out_shape, in_specs=[in_hbm] * 12 + [in_...]
where the time goes in v1:
time: 85.7 us; the launch traced here: 85.5 us
  Pallas kernels  84.2 us (98%)
  between operations  1.3 us (2%)
    pallas_call x1, Pallas kernels, tick(): pl.pallas_call(kernel, out_shape=out_shape, in_specs=[in_hbm] * 12 + [in_...  81.2 us
    pallas_call x1, Pallas kernels, hand_over(): pl.pallas_call(hand_over_kernel, out_shape=out_shape, in_specs=[in_hbm] *...  3.08 us

profile of v1, /device:TPU:1, one launch (start us, length us, event | category | flops | bytes accessed | tf_op | source)
XLA Modules:
  0.0 85.5 jit_solution(17758476425645996521)
XLA Ops:
  1.3 81.2 %tick.1 = (bf16[768,256]{1,0:T(8,128)(2,1)}, bf16[1024,256]{1,0:T(8,128)(2,1)}, bf16[768,256]{1,0:T(8,128)(2,1)}, bf16[1024,256]{1,0:T(8,128)(2,1)}, bf16[8,8,16...) custom-call(bf16[768,256]{1,0:T(8,128)(2,1)} %bitcast.18, bf16[1024,256]{1,0:T(8,128)(2,1)} %bitcast.15, ...), custom_call_target="tpu_custom_call" | custom-call | tf_op jit(solution)/shard_map/tick/pallas_call | solution.py:631
  82.5 3.1 %hand_over.1 = (bf16[1,768,256]{2,1,0:T(8,128)(2,1)}, bf16[1,1024,256]{2,1,0:T(8,128)(2,1)}, bf16[1,768,256]{2,1,0:T(8,128)(2,1)}, bf16[1,1024,256]{2,1,0:T(8,12...) custom-call(bf16[768,256]{1,0:T(8,128)(2,1)} %get-tuple-element.17.n, ...), custom_call_target="tpu_custom_call" | custom-call | tf_op jit(solution)/shard_map/hand_over/pallas_call | solution.py:696

commit v2 on v1

--- a/solution.py
+++ b/solution.py
@@ -15,6 +15,9 @@
 EDGE_CHUNK = 768
 NODE_CHUNK = 1024
 UNROLL = False
+A_ORDER = (4, 5, 3, 6, 2, 7, 1)
+B_ORDER = (4, 3, 5, 2, 6, 1, 7)
+OUT_CHUNK = 256
 VMEM_BYTES = 63 * 2**20
 
 
@@ -129,16 +132,26 @@
             barrier, inc=1, device_id={"phase": lax.rem(phase + step, phase_count)}, device_id_type=MESH
         )
 
+    groups = dom_count // (2 * Z_SIZE)
+    ypos = me // (2 * Z_SIZE)
+
+    def swing(n, size):
+        return size // 2 + (1 - 2 * lax.rem(n, 2)) * ((n + 1) // 2)
+
     def start_exchange(x):
         def one(k, carry):
-            other = lax.rem(me + k, dom_count)
+            other = (
+                lax.rem(ypos + swing(lax.rem(k // 2, groups), groups), groups) * (2 * Z_SIZE)
+                + lax.rem(zpos + swing(k // (2 * groups), Z_SIZE), Z_SIZE) * 2
+                + lax.rem(me + 1 + k, 2)
+            )
             pltpu.make_async_remote_copy(
                 out_slab.at[x, other], in_slab.at[x, me], x_send.at[x], x_recv.at[x],
                 device_id={"dom": other}, device_id_type=MESH,
             ).start()
             return carry
 
-        lax.fori_loop(1, dom_count, one, 0)
+        lax.fori_loop(0, dom_count - 1, one, 0)
         in_slab[x, me] = out_slab[x, me]
 
     def exchange_all(x):
@@ -183,19 +196,14 @@
     lax.fori_loop(0, mirror_tiles, build_want, 0)
 
     def pick_rows(x, rows):
-        def one(q, carry):
-            picked = dot(want_hot[rows_at(q, TILE), :], rows[0:own_tiles].reshape(node_dev, features) if len(rows.shape) == 3 else rows[...])
-            out_slab[x, pl.ds(pl.multiple_of(q * 16, 16), 16)] = to_slabs(picked)
-            return carry
-
-        lax.fori_loop(0, mirror_tiles, one, 0)
+        out_slab[x] = to_slabs(dot(want_hot[...], rows))
 
     operand(0).wait()
-    pick_rows(0, ns)
+    pick_rows(0, ns[...])
     pl.semaphore_wait(barrier, dom_count - 1 + 2)
     start_exchange(0)
     operand(1).wait()
-    pick_rows(1, nf)
+    pick_rows(1, nf[...])
     start_exchange(1)
 
     def build_edges(b, carry):
@@ -236,14 +244,13 @@
             total = total + jnp.broadcast_to(chosen, (TILE, features)) * block_sums[b]
         return total
 
-    def send_mirror_sums(x, first, count):
+    def put_mirror_sums(x, first, count):
         def one(q, carry):
             total = tile_total(own_tiles + q, first, count)
             out_slab[x, pl.ds(pl.multiple_of(q * 16, 16), 16)] = to_slabs(total)
             return carry
 
         lax.fori_loop(0, mirror_tiles, one, 0)
-        start_exchange(x)
 
     def own_sums(own, first, count):
         def one(k, carry):
@@ -251,6 +258,12 @@
             return carry
 
         lax.fori_loop(0, own_tiles, one, 0)
+
+    def edge_start(edges):
+        edge_pre[...] = dot(edges[...], w1[:features, :]) + ev[0:1, :]
+
+    def node_start(nodes):
+        node_pre[...] = dot(nodes[...], nw1[:features, :]) + nv[0:1, :]
 
     def edge_forward(edges, table, keep):
         def one(i, carry):
@@ -261,8 +274,11 @@
             from_recv = jnp.concatenate(
                 [fetch(recv_hot, i * per_chunk + j, table, 1) for j in range(per_chunk)], axis=0
             ).astype(BF16)
-            stacked = jnp.concatenate([edges[rows, :], from_send, from_recv], axis=1)
-            pre = dot(stacked, w1[...]) + ev[0:1, :]
+            stacked = jnp.concatenate([from_send, from_recv], axis=1)
+            if keep:
+                pre = edge_pre[rows, :] + dot(stacked, w1[features:, :])
+            else:
+                pre = dot(edges[rows, :], w1[:features, :]) + dot(stacked, w1[features:, :]) + ev[0:1, :]
             hidden = jnp.maximum(pre, 0.0).astype(BF16)
             normed, inverse = layer_norm(dot(hidden, w2[...]) + ev[1:2, :])
             message = live_rows(i) * (normed * ev[2:3, :] + ev[3:4, :])
@@ -287,8 +303,11 @@
             rows = rows_at(i, NODE_CHUNK)
             total = own[rows, :] + dot(want_hot_t[rows, :], returned)
             gathered = total.astype(BF16)
-            stacked = jnp.concatenate([nodes[rows, :], gathered], axis=1)
-            pre = dot(stacked, nw1[...]) + nv[0:1, :]
+            if keep:
+                pre = node_pre[rows, :] + dot(gathered, nw1[features:, :])
+            else:
+                stacked = jnp.concatenate([nodes[rows, :], gathered], axis=1)
+                pre = dot(stacked, nw1[...]) + nv[0:1, :]
             hidden = jnp.maximum(pre, 0.0).astype(BF16)
             normed, inverse = layer_norm(dot(hidden, nw2[...]) + nv[1:2, :])
             if keep:
@@ -307,21 +326,26 @@
 
     for n in (2, 3, 4, 5):
         operand(n).wait()
+    edge_start(es)
     table_s[own_tiles:] = wait_exchange(0).reshape(mirror_tiles, TILE, features)
     edge_forward(es, table_s, True)
-    send_mirror_sums(2, blocks, blocks)
+    put_mirror_sums(2, blocks, blocks)
+    start_exchange(2)
     own_sums(own_s, blocks, blocks)
 
     operand(6).wait()
     table_f[own_tiles:] = wait_exchange(1).reshape(mirror_tiles, TILE, features)
     edge_forward(ef, table_f, False)
-    send_mirror_sums(3, blocks, blocks)
     shift(0, new_edges, o_ne, 1).start()
+    put_mirror_sums(3, blocks, blocks)
+    start_exchange(3)
     own_sums(own_f, blocks, blocks)
 
     for n in (7, 8, 9, 10):
         operand(n).wait()
-    node_forward(ns, own_s, wait_exchange(2), True)
+    node_start(ns)
+    returned = wait_exchange(2)
+    node_forward(ns, own_s, returned, True)
 
     def node_back(i, carry):
         s_first, s_pre, s_gain, s_shift = carry
@@ -345,12 +369,12 @@
     for j in range(4):
         vec[4 + j:5 + j, :] = sums[j]
 
-    pick_rows(4, table_g)
+    pick_rows(4, table_g[0:own_tiles].reshape(node_dev, features))
     start_exchange(4)
 
     def start_a(which, grads, arrived, used):
         arrived[apos] = grads[apos]
-        for k in range(1, GROUP):
+        for k in A_ORDER:
             other, device = a_partner(k)
             pltpu.make_async_remote_copy(
                 grads.at[other, pl.ds(0, used)], arrived.at[apos, pl.ds(0, used)],
@@ -370,7 +394,7 @@
             total = total + arrived[k].astype(F32)
         sb[which] = total.astype(BF16).reshape(Z_SIZE, 16, features)
         rb[which, zpos] = sb[which, zpos]
-        for k in range(1, Z_SIZE):
+        for k in B_ORDER:
             other, device = b_partner(k)
             pltpu.make_async_remote_copy(
                 sb.at[which, other], rb.at[which, zpos], rb_s.at[which], rb_r.at[which],
@@ -390,7 +414,7 @@
             total = total + rb[which, k].astype(F32)
         fb[which] = total.astype(BF16)
         ab[which, zpos] = fb[which]
-        for k in range(1, Z_SIZE):
+        for k in B_ORDER:
             other, device = b_partner(k)
             pltpu.make_async_remote_copy(
                 fb.at[which], ab.at[which, zpos], gb_s.at[which], gb_r.at[which],
@@ -404,19 +428,27 @@
             device_id={"dom": b_partner(1)[1]}, device_id_type=MESH,
         )
 
+    z_used = ((3 * features) // GROUP // 16, Z_SIZE)
+
+    def own_share(which, out):
+        part = pl.ds(0, z_used[which])
+        return pltpu.make_async_copy(ab.at[which, part], out.at[apos, part], local_sem.at[which])
+
     def start_gather_a(which, out):
-        pltpu.make_async_copy(ab.at[which], out.at[apos], local_sem.at[which]).start()
-        for k in range(1, GROUP):
+        part = pl.ds(0, z_used[which])
+        own_share(which, out).start()
+        for k in A_ORDER:
             other, device = a_partner(k)
             pltpu.make_async_remote_copy(
-                ab.at[which], out.at[apos], ga_s.at[which], ga_r.at[which],
+                ab.at[which, part], out.at[apos, part], ga_s.at[which], ga_r.at[which],
                 device_id={"dom": device}, device_id_type=MESH,
             ).start()
 
     def all_gather_a(which, out):
         part = pl.ds(0, GROUP - 1)
+        used = pl.ds(0, z_used[which])
         return pltpu.make_async_remote_copy(
-            out.at[part], out.at[part], ga_s.at[which], ga_r.at[which],
+            out.at[part, used], out.at[part, used], ga_s.at[which], ga_r.at[which],
             device_id={"dom": a_partner(1)[1]}, device_id_type=MESH,
         )
 
@@ -482,15 +514,6 @@
     sums = lax.fori_loop(0, edge_chunks, edge_back, (zero_row,) * 4, unroll=UNROLL)
     for j in range(4):
         vec[j:j + 1, :] = sums[j]
-    send_mirror_sums(5, 0, 2 * blocks)
-
-    va[apos] = vec[...]
-    for k in range(1, GROUP):
-        other, device = a_partner(k)
-        pltpu.make_async_remote_copy(
-            vec, va.at[apos], v_s.at[0], v_r.at[0], device_id={"dom": device}, device_id_type=MESH
-        ).start()
-
     for part, rows in enumerate((es, sent_rows, recv_rows)):
         grad = dot_tn(rows[...], edge_first_grad[...]).astype(BF16)
         g_edge[2 * part] = grad[:TILE, :]
@@ -500,6 +523,9 @@
     g_edge[7] = grad[TILE:, :]
     start_a(1, g_edge, ra_edge, TILE)
 
+    put_mirror_sums(5, 0, 2 * blocks)
+    start_exchange(5)
+
     def edge_out(i, carry):
         rows = rows_at(i, EDGE_CHUNK)
         old_edges[rows, :] = (
@@ -510,29 +536,31 @@
     lax.fori_loop(0, edge_chunks, edge_out, 0, unroll=UNROLL)
     shift(2, old_edges, o_pe, phase_count - 1).start()
 
-    own_sums(own_s, 0, 2 * blocks)
     all_b(0).wait_recv()
     start_gather_b(0)
+
+    va[apos] = vec[...]
+    for k in range(1, GROUP):
+        other, device = a_partner(k)
+        pltpu.make_async_remote_copy(
+            vec, va.at[apos], v_s.at[0], v_r.at[0], device_id={"dom": device}, device_id_type=MESH
+        ).start()
+
+    own_sums(own_s, 0, 2 * blocks)
+    all_gather_b(0).wait_recv()
+    start_gather_a(0, o_gn)
     all_a(1, g_edge, ra_edge, TILE).wait_recv()
     start_b(1, ra_edge)
 
     returned = wait_exchange(5)
 
-    def node_out(i, carry):
-        rows = rows_at(i, NODE_CHUNK)
-        old_nodes[rows, :] = (
-            base[rows, :] + own_s[rows, :] + dot(want_hot_t[rows, :], returned)
-        ).astype(BF16)
+    for i in range(node_dev // OUT_CHUNK):
+        rows = pl.ds(i * OUT_CHUNK, OUT_CHUNK)
+        old_nodes[rows, :] = (base[rows, :] + own_s[rows, :] + dot(want_hot_t[rows, :], returned)).astype(BF16)
         shift(3, old_nodes.at[rows, :], o_pn.at[rows, :], phase_count - 1).start()
-        return carry
-
-    lax.fori_loop(0, node_chunks, node_out, 0, unroll=UNROLL)
 
     all_b(1).wait_recv()
     start_gather_b(1)
-    all_gather_b(0).wait_recv()
-    start_gather_a(0, o_gn)
-
     group_part = pl.ds(0, GROUP - 1)
     first_all = pltpu.make_async_remote_copy(
         va.at[group_part], va.at[group_part], v_s.at[0], v_r.at[0],
@@ -571,7 +599,7 @@
     for which, out in ((0, o_gn), (1, o_ge)):
         all_b(which).wait_send()
         all_gather_b(which).wait_send()
-        pltpu.make_async_copy(ab.at[which], out.at[apos], local_sem.at[which]).wait()
+        own_share(which, out).wait()
         all_gather_a(which, out).wait_send()
         all_gather_a(which, out).wait_recv()
     shift(0, new_edges, o_ne, 1).wait()

time: 85.7 us -> 80.4 us (0.938)
  Pallas kernels: 84.2 us -> 78.9 us
    pallas_call x1, Pallas kernels: 81.2 us -> 75.9 us  [tick(): pl.pallas_call(kernel, out_shape=out_shape, in_specs=[in_hbm] * 12 + [in_...]
where the time goes in v2:
time: 80.4 us; the launch traced here: 80.2 us
  Pallas kernels  78.9 us (98%)
  between operations  1.3 us (2%)
    pallas_call x1, Pallas kernels, tick(): pl.pallas_call(kernel, out_shape=out_shape, in_specs=[in_hbm] * 12 + [in_...  75.9 us
    pallas_call x1, Pallas kernels, hand_over(): pl.pallas_call(hand_over_kernel, out_shape=out_shape, in_specs=[in_hbm] *...  3.08 us

profile of v2, /device:TPU:1, one launch (start us, length us, event | category | flops | bytes accessed | tf_op | source)
XLA Modules:
  0.0 80.2 jit_solution(2955725349032165195)
XLA Ops:
  1.3 75.9 %tick.1 = (bf16[768,256]{1,0:T(8,128)(2,1)}, bf16[1024,256]{1,0:T(8,128)(2,1)}, bf16[768,256]{1,0:T(8,128)(2,1)}, bf16[1024,256]{1,0:T(8,128)(2,1)}, bf16[8,8,16...) custom-call(bf16[768,256]{1,0:T(8,128)(2,1)} %bitcast.18, bf16[1024,256]{1,0:T(8,128)(2,1)} %bitcast.15, ...), custom_call_target="tpu_custom_call" | custom-call | tf_op jit(solution)/shard_map/tick/pallas_call | solution.py:659
  77.2 3.1 %hand_over.1 = (bf16[1,768,256]{2,1,0:T(8,128)(2,1)}, bf16[1,1024,256]{2,1,0:T(8,128)(2,1)}, bf16[1,768,256]{2,1,0:T(8,128)(2,1)}, bf16[1,1024,256]{2,1,0:T(8,12...) custom-call(bf16[768,256]{1,0:T(8,128)(2,1)} %get-tuple-element.17.n, ...), custom_call_target="tpu_custom_call" | custom-call | tf_op jit(solution)/shard_map/hand_over/pallas_call | solution.py:724

commit v3 on v2

--- a/solution.py
+++ b/solution.py
@@ -151,7 +151,7 @@
             ).start()
             return carry
 
-        lax.fori_loop(0, dom_count - 1, one, 0)
+        lax.fori_loop(0, dom_count - 1, one, 0, unroll=9)
         in_slab[x, me] = out_slab[x, me]
 
     def exchange_all(x):
@@ -193,7 +193,7 @@
             want_hot[rows_at(b, TILE), j * TILE:(j + 1) * TILE] = (col == lane_float + float(j * TILE)).astype(F32).astype(BF16)
         return carry
 
-    lax.fori_loop(0, mirror_tiles, build_want, 0)
+    lax.fori_loop(0, mirror_tiles, build_want, 0, unroll=True)
 
     def pick_rows(x, rows):
         out_slab[x] = to_slabs(dot(want_hot[...], rows))
@@ -250,7 +250,7 @@
             out_slab[x, pl.ds(pl.multiple_of(q * 16, 16), 16)] = to_slabs(total)
             return carry
 
-        lax.fori_loop(0, mirror_tiles, one, 0)
+        lax.fori_loop(0, mirror_tiles, one, 0, unroll=True)
 
     def own_sums(own, first, count):
         def one(k, carry):
@@ -547,10 +547,10 @@
         ).start()
 
     own_sums(own_s, 0, 2 * blocks)
+    all_a(1, g_edge, ra_edge, TILE).wait_recv()
+    start_b(1, ra_edge)
     all_gather_b(0).wait_recv()
     start_gather_a(0, o_gn)
-    all_a(1, g_edge, ra_edge, TILE).wait_recv()
-    start_b(1, ra_edge)
 
     returned = wait_exchange(5)
 

time: 80.4 us -> 80 us (level)
  no operation moved by 1% of the time
where the time goes in v3:
time: 80 us; the launch traced here: 79.8 us
  Pallas kernels  78.3 us (98%)
  between operations  1.46 us (2%)
    pallas_call x1, Pallas kernels, tick(): pl.pallas_call(kernel, out_shape=out_shape, in_specs=[in_hbm] * 12 + [in_...  75.2 us
    pallas_call x1, Pallas kernels, hand_over(): pl.pallas_call(hand_over_kernel, out_shape=out_shape, in_specs=[in_hbm] *...  3.08 us

profile of v3, /device:TPU:1, one launch (start us, length us, event | category | flops | bytes accessed | tf_op | source)
XLA Modules:
  0.0 79.8 jit_solution(15693630500682907857)
XLA Ops:
  1.3 75.2 %tick.1 = (bf16[768,256]{1,0:T(8,128)(2,1)}, bf16[1024,256]{1,0:T(8,128)(2,1)}, bf16[768,256]{1,0:T(8,128)(2,1)}, bf16[1024,256]{1,0:T(8,128)(2,1)}, bf16[8,8,16...) custom-call(bf16[768,256]{1,0:T(8,128)(2,1)} %bitcast.18, bf16[1024,256]{1,0:T(8,128)(2,1)} %bitcast.15, ...), custom_call_target="tpu_custom_call" | custom-call | tf_op jit(solution)/shard_map/tick/pallas_call | solution.py:659
  76.5 3.1 %hand_over.1 = (bf16[1,768,256]{2,1,0:T(8,128)(2,1)}, bf16[1,1024,256]{2,1,0:T(8,128)(2,1)}, bf16[1,768,256]{2,1,0:T(8,128)(2,1)}, bf16[1,1024,256]{2,1,0:T(8,12...) custom-call(bf16[768,256]{1,0:T(8,128)(2,1)} %get-tuple-element.17.n, ...), custom_call_target="tpu_custom_call" | custom-call | tf_op jit(solution)/shard_map/hand_over/pallas_call | solution.py:724
